TPU v7x, 32 devices: a whole 2x2x4 slice. The times are simulated.
32 devices in a mesh: region: 8 (over z, y), rep: 4 (over x, core).
Axes of the slice: x: 2, y: 2, z: 4, core: 2. Of those that a mesh axis runs over, the one named last changes fastest.
Arguments:
- unit_cost: float32 [16, 131072], P(None, ('region', 'rep')), may hold values from -6 to 6
- start_primal: float32 [16, 131072], P(None, ('region', 'rep')), may hold values from 0 to 0.125
- start_dual: float32 [65536], P('region'), may hold values from 0 to 1
- quota_bound: float32 [65536], P('region'), may hold values from 2 to 6
- person_slot: int32 [131072], P(('region', 'rep')), may hold values from 0 to 1023
- cell_lists: int32 [8, 8, 128], P('region'), may hold values from 0 to 511
Outputs:
- primal: float32 [16, 131072], P(None, ('region', 'rep'))
- dual: float32 [65536], P('region')
Inputs may be any that keep to these rules, and one draw needn't show every extreme that they name: person_slot = d * 128 + j names slot j of the person's region's list toward owner block d.
All inputs are finite; a program needn't handle non-finite values.
Results may differ from a plain program's by a relative error of at most 0.0003.
Values sent between devices are 32-bit elements; how exact they have to be, the bound alone decides.
No kernel may reach another device: no remote copies, remote signals or barrier semaphores. Data moves between devices by JAX's collectives and lax.ppermute only.
A program may use at most 64 MiB of HBM per device.

v0:
```python
import jax
import jax.numpy as jnp
from jax import lax
from jax.sharding import PartitionSpec as P

ITERS = 2
BISECT = 30
PRIMAL_STEP = 0.5
DUAL_STEP = 0.25


def project_simplex(values):
    largest = jnp.max(values, axis=0)

    def bisect_once(repeat, bounds):
        low_end, high_end = bounds
        middle = 0.5 * (low_end + high_end)
        mass_sum = jnp.sum(jnp.maximum(values - middle, 0.0), axis=0)
        above = mass_sum > 1.0
        return (jnp.where(above, middle, low_end), jnp.where(above, high_end, middle))

    low_end, high_end = lax.fori_loop(0, BISECT, bisect_once, (largest - 1.0, largest))
    middle = 0.5 * (low_end + high_end)
    return jnp.maximum(values - middle, 0.0)


def local(unit_cost, start_primal, start_dual, quota_bound, person_slot, cell_lists):
    options = unit_cost.shape[0]
    regions = lax.axis_size("region")
    list_len = cell_lists.shape[2]
    groups = quota_bound.shape[0] // options
    slot_count = regions * list_len
    own_lists = cell_lists[0]
    primal = start_primal
    dual = start_dual
    for repeat in range(ITERS):
        dual_rows = dual.reshape(groups, options)
        picked = jnp.take(dual_rows, own_lists.reshape(-1), axis=0).reshape(
            regions, list_len * options
        )
        slot_arrived = lax.all_to_all(picked, "region", split_axis=0, concat_axis=0, tiled=True)
        prices = slot_arrived.reshape(slot_count, options)
        adjoint = jnp.take(prices, person_slot, axis=0).T
        fresh = project_simplex(primal - PRIMAL_STEP * (unit_cost + adjoint))
        partial_rows = jax.ops.segment_sum(
            (2.0 * fresh - primal).T, person_slot, num_segments=slot_count
        )
        partial_rows = partial_rows.reshape(regions, list_len * options)
        summed = lax.psum(partial_rows, "rep")
        arrived = lax.all_to_all(summed, "region", split_axis=0, concat_axis=0, tiled=True)
        block_sum = jax.ops.segment_sum(
            arrived.reshape(slot_count, options), own_lists.reshape(-1), num_segments=groups
        )
        applied = block_sum.reshape(-1)
        dual = jnp.maximum(dual + DUAL_STEP * (applied - quota_bound), 0.0)
        primal = fresh
    return (primal, dual)


def solution(mesh):
    placed = (
        P(None, ("region", "rep")),
        P(None, ("region", "rep")),
        P("region"),
        P("region"),
        P(("region", "rep")),
        P("region", None, None),
    )
    return jax.shard_map(
        local,
        mesh=mesh,
        in_specs=placed,
        out_specs=(P(None, ("region", "rep")), P("region")),
        check_vma=False,
    )
```

profile of v0, /device:TPU:0, one launch (start us, length us, event | category | flops | bytes accessed | tf_op | source)
XLA Modules:
  0.0 246.2 jit_solution(10379357901981070034)
XLA Ops:
  7.2 0.7 compare_and_fusion.1
  8.6 0.9 reshape.64
  9.5 2.8 %gather_fusion = f32[1024,16]{1,0:T(8,128)S(1)} fusion(f32[512,16]{1,0:T(8,128)S(1)} %reshape.64, s32[1024]{0:T(1024)S(1)} %fusion.29), kind=kCustom, calls=%fused_computation.clone | custom fusion | bytes 135168 | tf_op jit(solution)/shard_map/jit(_take)/gather | solution.py:38
  12.5 0.9 all_to_all.32
  13.4 7.3 %all-to-all-start = ((f32[8,1,2048]{2,1,0:T(1,128)}), f32[8,1,2048]{2,1,0:T(1,128)S(1)}, u32[]{:S(2)}, u32[]{:S(2)}) async-start(f32[8,1,2048]{2,1,0:T(1,128)} %all_to_all.32), calls=%async_computation | async-start | bytes 131072 | tf_op jit(solution)/shard_map/all_to_all | solution.py:41
  20.7 2.0 copy.23
  22.7 1.9 copy.24
  24.6 2.9 %all-to-all-done = f32[8,1,2048]{2,1,0:T(1,128)S(1)} async-done(((f32[8,1,2048]{2,1,0:T(1,128)}), f32[8,1,2048]{2,1,0:T(1,128)S(1)}, u32[]{:S(2)}, u32[]{:S(2)}) %all-to-all-start) | async-done | bytes 65568 | tf_op jit(solution)/shard_map/all_to_all | solution.py:41
  27.9 14.1 %gather_fusion.1 = f32[4096,16]{1,0:T(8,128)} fusion(f32[1024,16]{1,0:T(8,128)S(1)} %reshape.65, s32[4096]{0:T(1024)S(1)} %fusion.28), kind=kCustom, calls=%fused_computation.1.clone | custom fusion | bytes 540672 | tf_op jit(solution)/shard_map/jit(_take)/gather | solution.py:43
  42.0 3.5 %fusion.32 = (f32[4096]{0:T(1024)S(1)}, f32[16,4096]{0,1:T(8,128)S(1)}) fusion(f32[16,4096]{0,1:T(8,128)} %copy.24, f32[16,4096]{0,1:T(8,128)} %copy.23, f32[4096,16]{1,0:T(8,128)} %gather_fusion.1, pred[4096]{0:T(1024)(128)(4,1)S(1)} %compare_and_fusion), kind=kLoop, calls=%fused_computation.61 | loop fusion | flops 323584 | bytes 1069056 | tf_op jit(solution)/shard_map/reduce_max | solution.py:13
  46.0 4.1 %while.24 = (s32[]{:T(128)}, f32[4096]{0:T(1024)S(1)}, f32[4096]{0:T(1024)S(1)}, f32[16,4096]{1,0:T(8,128)S(1)}, s32[]{:T(128)}) while((s32[]{:T(128)}, f32[4096]{0:T(1024)S(1)}, f32[4096]{0:T(1024)S(1)}, f32[16,4096]{1,0:T(8,128)S(1)}, s32[]{:T(128)}) %tuple.54), condition=%wide.region_3.6_spmd, body=%wide.region_1.0_spmd.sunk | while | flops 229378 | bytes 499773 | solution.py:22
  50.1 24.9 %scatter_custom_fusion = f32[1024,16]{1,0:T(8,128)S(1)} fusion(s32[4096]{0:T(1024)S(1)} %copy-done.4, f32[16,4096]{0,1:T(8,128)} %copy.24, f32[16,4096]{0,1:T(8,128)S(1)} %get-tuple-element.107, f32[]{:T(128)} %constant.48.clone.1, f32[]{:T(128)} %constant.47.clone.1, f32[4096]{0:T(1024)S(1)} %add_multiply_fusion.3), kind=kCustom, calls=%fused_computation.23 | custom fusion | flops 327680 | bytes 4277760 | tf_op jit(solution)/shard_map/scatter-add | solution.py:45
  75.1 0.9 all_to_all.26
  76.1 29.6 %all-reduce.3.cloned.1.call-done = f32[8,1,2048]{2,0,1:T(8,128)} async-done(((f32[8,1,2048]{2,0,1:T(8,128)}), f32[8,1,2048]{2,0,1:T(8,128)}) %all-reduce.3.cloned.1.call-update) | async-done | bytes 65552 | tf_op jit(solution)/shard_map/psum | solution.py:49
  105.7 0.9 copy.27
  106.6 12.2 %all_to_all.38 = f32[8,1,2048]{2,1,0:T(1,128)S(1)} all-to-all(f32[8,1,2048]{2,1,0:T(1,128)S(1)} %copy.27), channel_id=1, replica_groups=mesh['region'=8,'rep'=4] {'region'}, dimensions={0} | all-to-all | bytes 131072 | tf_op jit(solution)/shard_map/all_to_all | solution.py:50
  119.2 6.2 %scatter_custom_fusion.1 = f32[512,16]{1,0:T(8,128)S(1)} fusion(s32[1024]{0:T(1024)} %bitcast.23, f32[1024,16]{1,0:T(8,128)S(1)} %reshape.120, f32[]{:T(128)} %constant.47.clone.1), kind=kCustom, calls=%fused_computation.46 | custom fusion | flops 16384 | bytes 33280 | tf_op jit(solution)/shard_map/scatter-add | solution.py:51
  125.7 2.8 %gather_fusion.2 = f32[1024,16]{1,0:T(8,128)S(1)} fusion(f32[512,16]{1,0:T(8,128)S(1)} %reshape.69, s32[1024]{0:T(1024)S(1)} %fusion.29), kind=kCustom, calls=%fused_computation.2.clone | custom fusion | bytes 135168 | tf_op jit(solution)/shard_map/jit(_take)/gather | solution.py:38
  128.9 9.3 %all_to_all.39 = f32[8,1,2048]{2,1,0:T(1,128)S(1)} all-to-all(f32[8,1,2048]{2,1,0:T(1,128)S(1)} %all_to_all.33), channel_id=1, replica_groups=mesh['region'=8,'rep'=4] {'region'}, dimensions={0} | all-to-all | bytes 131072 | tf_op jit(solution)/shard_map/all_to_all | solution.py:41
  138.6 14.1 %gather_fusion.3 = f32[4096,16]{1,0:T(8,128)} fusion(f32[1024,16]{1,0:T(8,128)S(1)} %reshape.70, s32[4096]{0:T(1024)S(1)} %fusion.28), kind=kCustom, calls=%fused_computation.3.clone | custom fusion | bytes 540672 | tf_op jit(solution)/shard_map/jit(_take)/gather | solution.py:43
  152.7 4.9 %fusion.30 = (f32[4096]{0:T(1024)S(1)}, f32[16,4096]{0,1:T(8,128)}) fusion(f32[16,4096]{0,1:T(8,128)} %copy.23, f32[4096,16]{1,0:T(8,128)} %gather_fusion.3, pred[4096]{0:T(1024)(128)(4,1)S(1)} %compare_and_fusion, f32[16,4096]{0,1:T(8,128)S(1)} %get-tuple-element.107, f32[4096]{0:T(1024)S(1)} %add_multiply_fusion.3), kind=kLoop, calls=%fused_computation.60 | loop fusion | flops 454656 | bytes 1085440 | tf_op jit(solution)/shard_map/reduce_max | solution.py:13
  157.6 2.2 copy.30
  159.7 4.1 %while.25 = (s32[]{:T(128)}, f32[4096]{0:T(1024)S(1)}, f32[4096]{0:T(1024)S(1)}, f32[16,4096]{1,0:T(8,128)S(1)}, s32[]{:T(128)}) while((s32[]{:T(128)}, f32[4096]{0:T(1024)S(1)}, f32[4096]{0:T(1024)S(1)}, f32[16,4096]{1,0:T(8,128)S(1)}, s32[]{:T(128)}) %tuple.57), condition=%wide.region_10.13_spmd, body=%wide.region_8.12_spmd.sunk | while | flops 229378 | bytes 499773 | solution.py:22
  163.8 25.5 %scatter_custom_fusion.2 = f32[1024,16]{1,0:T(8,128)S(1)} fusion(s32[4096]{0:T(1024)S(1)} %copy-done.4, f32[16,4096]{0,1:T(8,128)S(1)} %get-tuple-element.107, f32[]{:T(128)} %constant.48.clone.1, f32[]{:T(128)} %constant.47.clone.1, f32[4096]{0:T(1024)S(1)} %add_multiply_fusion.3, f32[16,4096]{0,1:T(8,128)} %get-tuple-element.105, ...), kind=kCustom, calls=%fused_computation.18 | custom fusion | flops 458752 | bytes 4294144 | tf_op jit(solution)/shard_map/scatter-add | solution.py:45
  189.4 0.9 all_to_all.30
  190.3 27.8 %all-reduce.5.cloned.1.call-done = f32[8,1,2048]{2,0,1:T(8,128)} async-done(((f32[8,1,2048]{2,0,1:T(8,128)}), f32[8,1,2048]{2,0,1:T(8,128)}) %all-reduce.5.cloned.1.call-update) | async-done | bytes 65552 | tf_op jit(solution)/shard_map/psum | solution.py:49
  218.1 1.5 copy.31
  219.6 5.5 %all-to-all-start.3 = ((f32[8,1,2048]{2,1,0:T(1,128)}), f32[8,1,2048]{2,1,0:T(1,128)S(1)}, u32[]{:S(2)}, u32[]{:S(2)}) async-start(f32[8,1,2048]{2,1,0:T(1,128)} %copy.31), calls=%async_computation.3 | async-start | bytes 131072 | tf_op jit(solution)/shard_map/all_to_all | solution.py:50
  225.1 1.9 subtract_maximum_fusion
  227.0 1.3 copy.32
  228.3 3.7 %all-to-all-done.3 = f32[8,1,2048]{2,1,0:T(1,128)S(1)} async-done(((f32[8,1,2048]{2,1,0:T(1,128)}), f32[8,1,2048]{2,1,0:T(1,128)S(1)}, u32[]{:S(2)}, u32[]{:S(2)}) %all-to-all-start.3) | async-done | bytes 65568 | tf_op jit(solution)/shard_map/all_to_all | solution.py:50
  232.4 6.2 %scatter_custom_fusion.3 = f32[512,16]{1,0:T(8,128)S(1)} fusion(s32[1024]{0:T(1024)} %bitcast.24, f32[1024,16]{1,0:T(8,128)S(1)} %reshape.136, f32[]{:T(128)} %constant.47.clone.1), kind=kCustom, calls=%fused_computation.44 | custom fusion | flops 16384 | bytes 33280 | tf_op jit(solution)/shard_map/scatter-add | solution.py:51
  (338 shorter events, 9.6 us)
Async XLA Ops:
  9.4 11.3 %copy-start.4 = (s32[4096]{0:T(1024)S(1)}, s32[4096]{0:T(1024)}, u32[]{:S(2)}) copy-start(s32[4096]{0:T(1024)} %param.18) | copy-start | bytes 49156
  9.4 11.3 %copy-start = (f32[16,4096]{1,0:T(8,128)S(1)}, f32[16,4096]{1,0:T(8,128)}, u32[]{:S(2)}) copy-start(f32[16,4096]{1,0:T(8,128)} %param.14) | copy-start | bytes 786436
  12.3 10.4 %copy-start.1 = (f32[16,4096]{1,0:T(8,128)S(1)}, f32[16,4096]{1,0:T(8,128)}, u32[]{:S(2)}) copy-start(f32[16,4096]{1,0:T(8,128)} %param.15) | copy-start | bytes 786436
  13.4 14.2 %all-to-all-start = ((f32[8,1,2048]{2,1,0:T(1,128)}), f32[8,1,2048]{2,1,0:T(1,128)S(1)}, u32[]{:S(2)}, u32[]{:S(2)}) async-start(f32[8,1,2048]{2,1,0:T(1,128)} %all_to_all.32), calls=%async_computation | async-start | bytes 131072 | tf_op jit(solution)/shard_map/all_to_all | solution.py:41
  20.6 85.0 %all-reduce.3.cloned.1.call-start = ((), (), s32[]{:S(2)}) async-start(), calls=%async_computation.4 | async-start | bytes 131072 | tf_op jit(solution)/shard_map/psum | solution.py:49
  75.1 50.4 %copy-start.2 = (f32[8192]{0:T(1024)S(1)}, f32[8192]{0:T(1024)}, u32[]{:S(2)}) copy-start(f32[8192]{0:T(1024)} %param.16) | copy-start | bytes 98308
  75.1 50.4 %copy-start.3 = (f32[8192]{0:T(1024)S(1)}, f32[8192]{0:T(1024)}, u32[]{:S(2)}) copy-start(f32[8192]{0:T(1024)} %param.17) | copy-start | bytes 98308
  76.0 142.0 %all-reduce.5.cloned.1.call-start = ((), (), s32[]{:S(2)}) async-start(), calls=%async_computation.5 | async-start | bytes 131072 | tf_op jit(solution)/shard_map/psum | solution.py:49
  219.6 12.4 %all-to-all-start.3 = ((f32[8,1,2048]{2,1,0:T(1,128)}), f32[8,1,2048]{2,1,0:T(1,128)S(1)}, u32[]{:S(2)}, u32[]{:S(2)}) async-start(f32[8,1,2048]{2,1,0:T(1,128)} %copy.31), calls=%async_computation.3 | async-start | bytes 131072 | tf_op jit(solution)/shard_map/all_to_all | solution.py:50
Sparse Core Ops, SparseCore 0:
  76.2 29.4 all-reduce.2
  190.4 27.6 all-reduce.4
where the time goes:
time: 247 us; the launch traced here: 246 us
  other arithmetic  81.1 us (33%)
  waiting for transfers between devices  64 us (26%)
  local copies, waits for them, and re-layouts  49.3 us (20%)
  blocking collectives  21.5 us (9%)
  between operations  14.3 us (6%)
  starting transfers between devices  12.9 us (5%)
  loops' own time  3.07 us (1%)
    psum x2, waiting for transfers between devices, local(): summed = lax.psum(partial_rows, 'rep')  57.4 us
    scatter-add x2, other arithmetic, local(): jax.ops.segment_sum((2.0 * fresh - primal).T, person_slot, num_segments=s...  50.5 us
    gather x2, local copies, waits for them, and re-layouts, local(): adjoint = jnp.take(prices, person_slot, axis=0).T  28.2 us
    scatter-add x2, other arithmetic, local(): jax.ops.segment_sum(arrived.reshape(slot_count, options), own_lists.resha...  12.4 us
    all_to_all x1, blocking collectives, local(): lax.all_to_all(summed, 'region', split_axis=0, concat_axis=0, tiled=True)  12.2 us
    all_to_all x1, blocking collectives, local(): lax.all_to_all(picked, 'region', split_axis=0, concat_axis=0, tiled=True)  9.29 us
    reduce_max x2, other arithmetic, project_simplex(): largest = jnp.max(values, axis=0)  8.33 us
    all_to_all x1, starting transfers between devices, local(): lax.all_to_all(picked, 'region', split_axis=0, concat_axis=0, tiled=True)  7.28 us
  transfers between devices with their start and end apart: 4, of which 4 were waited for; matrix products, arithmetic and copies ran while one was open for 3% of the time, Pallas kernels for 0%

commit v1 on v0

--- a/solution.py
+++ b/solution.py
@@ -46,7 +46,7 @@
             (2.0 * fresh - primal).T, person_slot, num_segments=slot_count
         )
         partial_rows = partial_rows.reshape(regions, list_len * options)
-        summed = lax.psum(partial_rows, "rep")
+        summed = jnp.sum(lax.all_gather(partial_rows, "rep"), 0)
         arrived = lax.all_to_all(summed, "region", split_axis=0, concat_axis=0, tiled=True)
         block_sum = jax.ops.segment_sum(
             arrived.reshape(slot_count, options), own_lists.reshape(-1), num_segments=groups

time: 247 us -> 180 us (0.73)
  waiting for transfers between devices: 64 us -> 6.62 us
  between operations: 14.3 us -> 0.95 us
  blocking collectives: 21.5 us -> 30.6 us
  local copies, waits for them, and re-layouts: 49.3 us -> 46.3 us
    psum x2 -> x0, waiting for transfers between devices: 57.4 us -> none  [local(): summed = lax.psum(partial_rows, 'rep')]
    all_gather x0 -> x2, blocking collectives: none -> 11.6 us  [local(): summed = jnp.sum(lax.all_gather(partial_rows, 'rep'), 0)]
    all_to_all x1, blocking collectives: 12.2 us -> 9.71 us  [local(): lax.all_to_all(summed, 'region', split_axis=0, concat_axis=0, tiled=True)]
  transfers between devices with their start and end apart: 4 -> 2, of which waited for: 4 -> 2; matrix products, arithmetic and copies ran while one was open for 3% -> 4% of each run, Pallas kernels for 0% -> 0%
where the time goes in v1:
time: 180 us; the launch traced here: 179 us
  other arithmetic  81.2 us (45%)
  local copies, waits for them, and re-layouts  46.3 us (26%)
  blocking collectives  30.6 us (17%)
  starting transfers between devices  10.6 us (6%)
  waiting for transfers between devices  6.62 us (4%)
  loops' own time  3.07 us (2%)
    scatter-add x2, other arithmetic, local(): jax.ops.segment_sum((2.0 * fresh - primal).T, person_slot, num_segments=s...  50.5 us
    gather x2, local copies, waits for them, and re-layouts, local(): adjoint = jnp.take(prices, person_slot, axis=0).T  28.2 us
    scatter-add x2, other arithmetic, local(): jax.ops.segment_sum(arrived.reshape(slot_count, options), own_lists.resha...  12.4 us
    all_gather x2, blocking collectives, local(): summed = jnp.sum(lax.all_gather(partial_rows, 'rep'), 0)  11.6 us
    all_to_all x1, blocking collectives, local(): lax.all_to_all(summed, 'region', split_axis=0, concat_axis=0, tiled=True)  9.71 us
    all_to_all x1, blocking collectives, local(): lax.all_to_all(picked, 'region', split_axis=0, concat_axis=0, tiled=True)  9.29 us
    reduce_max x2, other arithmetic, project_simplex(): largest = jnp.max(values, axis=0)  8.33 us
    all_to_all x1, starting transfers between devices, local(): lax.all_to_all(picked, 'region', split_axis=0, concat_axis=0, tiled=True)  7.28 us
  transfers between devices with their start and end apart: 2, of which 2 were waited for; matrix products, arithmetic and copies ran while one was open for 4% of the time, Pallas kernels for 0%

profile of v1, /device:TPU:0, one launch (start us, length us, event | category | flops | bytes accessed | tf_op | source)
XLA Modules:
  0.0 179.3 jit_solution(13863019633205259745)
XLA Ops:
  0.6 0.7 compare_and_fusion.1
  1.3 0.7 fusion.29
  2.0 0.9 reshape.58
  2.9 2.8 %gather_fusion = f32[1024,16]{1,0:T(8,128)S(1)} fusion(f32[512,16]{1,0:T(8,128)S(1)} %reshape.58, s32[1024]{0:T(1024)S(1)} %fusion.29), kind=kCustom, calls=%fused_computation.clone | custom fusion | bytes 135168 | tf_op jit(solution)/shard_map/jit(_take)/gather | solution.py:38
  6.0 0.9 all_to_all.32
  6.8 7.3 %all-to-all-start = ((f32[8,1,2048]{2,1,0:T(1,128)}), f32[8,1,2048]{2,1,0:T(1,128)S(1)}, u32[]{:S(2)}, u32[]{:S(2)}) async-start(f32[8,1,2048]{2,1,0:T(1,128)} %all_to_all.32), calls=%async_computation | async-start | bytes 131072 | tf_op jit(solution)/shard_map/all_to_all | solution.py:41
  14.1 2.0 %copy.23 = f32[16,4096]{0,1:T(8,128)} copy(f32[16,4096]{1,0:T(8,128)S(1)} %copy-done) | data formatting | bytes 524288 | tf_op args[0]
  16.1 1.9 %copy.24 = f32[16,4096]{0,1:T(8,128)} copy(f32[16,4096]{1,0:T(8,128)S(1)} %copy-done.1) | data formatting | bytes 524288 | tf_op args[1]
  18.0 3.0 %all-to-all-done = f32[8,1,2048]{2,1,0:T(1,128)S(1)} async-done(((f32[8,1,2048]{2,1,0:T(1,128)}), f32[8,1,2048]{2,1,0:T(1,128)S(1)}, u32[]{:S(2)}, u32[]{:S(2)}) %all-to-all-start) | async-done | bytes 65568 | tf_op jit(solution)/shard_map/all_to_all | solution.py:41
  21.4 14.1 %gather_fusion.1 = f32[4096,16]{1,0:T(8,128)} fusion(f32[1024,16]{1,0:T(8,128)S(1)} %reshape.59, s32[4096]{0:T(1024)S(1)} %fusion.28), kind=kCustom, calls=%fused_computation.1.clone | custom fusion | bytes 540672 | tf_op jit(solution)/shard_map/jit(_take)/gather | solution.py:43
  35.5 3.5 %fusion.32 = (f32[4096]{0:T(1024)S(1)}, f32[16,4096]{0,1:T(8,128)S(1)}) fusion(f32[16,4096]{0,1:T(8,128)} %copy.24, f32[16,4096]{0,1:T(8,128)} %copy.23, f32[4096,16]{1,0:T(8,128)} %gather_fusion.1, pred[4096]{0:T(1024)(128)(4,1)S(1)} %compare_and_fusion), kind=kLoop, calls=%fused_computation.61 | loop fusion | flops 323584 | bytes 1069056 | tf_op jit(solution)/shard_map/reduce_max | solution.py:13
  38.9 0.6 copy.25
  39.5 4.1 %while.24 = (s32[]{:T(128)}, f32[4096]{0:T(1024)S(1)}, f32[4096]{0:T(1024)S(1)}, f32[16,4096]{1,0:T(8,128)S(1)}, s32[]{:T(128)}) while((s32[]{:T(128)}, f32[4096]{0:T(1024)S(1)}, f32[4096]{0:T(1024)S(1)}, f32[16,4096]{1,0:T(8,128)S(1)}, s32[]{:T(128)}) %tuple.54), condition=%wide.region_3.6_spmd, body=%wide.region_1.0_spmd.sunk | while | flops 229378 | bytes 499773 | solution.py:22
  43.6 24.9 %scatter_custom_fusion = f32[1024,16]{1,0:T(8,128)S(1)} fusion(s32[4096]{0:T(1024)S(1)} %copy-done.4, f32[16,4096]{0,1:T(8,128)} %copy.24, f32[16,4096]{0,1:T(8,128)S(1)} %get-tuple-element.107, f32[]{:T(128)} %constant.48.clone.1, f32[]{:T(128)} %constant.10.clone.1, f32[4096]{0:T(1024)S(1)} %add_multiply_fusion.3), kind=kCustom, calls=%fused_computation.23 | custom fusion | flops 327680 | bytes 4277760 | tf_op jit(solution)/shard_map/scatter-add | solution.py:45
  68.9 5.8 %all_gather.6 = f32[4,8,2048]{2,1,0:T(8,128)S(1)} all-gather(f32[1,8,2048]{2,1,0:T(8,128)S(1)} %all_gather_reshape.6), channel_id=1, replica_groups=mesh['region'=8,'rep'=4] {'rep'}, dimensions={0}, use_global_device_ids=true | all-gather | bytes 327680 | tf_op jit(solution)/shard_map/all_gather | solution.py:49
  74.7 9.7 %all_to_all.38 = f32[8,1,2048]{2,1,0:T(1,128)S(1)} all-to-all(f32[8,1,2048]{2,1,0:T(1,128)S(1)} %all_to_all.26), channel_id=1, replica_groups=mesh['region'=8,'rep'=4] {'region'}, dimensions={0} | all-to-all | bytes 131072 | tf_op jit(solution)/shard_map/all_to_all | solution.py:50
  84.8 6.2 %scatter_custom_fusion.1 = f32[512,16]{1,0:T(8,128)S(1)} fusion(s32[1024]{0:T(1024)} %bitcast.23, f32[1024,16]{1,0:T(8,128)S(1)} %reshape.110, f32[]{:T(128)} %constant.10.clone.1), kind=kCustom, calls=%fused_computation.46 | custom fusion | flops 16384 | bytes 33280 | tf_op jit(solution)/shard_map/scatter-add | solution.py:51
  91.3 2.8 %gather_fusion.2 = f32[1024,16]{1,0:T(8,128)S(1)} fusion(f32[512,16]{1,0:T(8,128)S(1)} %reshape.62, s32[1024]{0:T(1024)S(1)} %fusion.29), kind=kCustom, calls=%fused_computation.2.clone | custom fusion | bytes 135168 | tf_op jit(solution)/shard_map/jit(_take)/gather | solution.py:38
  94.6 9.3 %all_to_all.39 = f32[8,1,2048]{2,1,0:T(1,128)S(1)} all-to-all(f32[8,1,2048]{2,1,0:T(1,128)S(1)} %all_to_all.33), channel_id=1, replica_groups=mesh['region'=8,'rep'=4] {'region'}, dimensions={0} | all-to-all | bytes 131072 | tf_op jit(solution)/shard_map/all_to_all | solution.py:41
  104.2 14.1 %gather_fusion.3 = f32[4096,16]{1,0:T(8,128)} fusion(f32[1024,16]{1,0:T(8,128)S(1)} %reshape.63, s32[4096]{0:T(1024)S(1)} %fusion.28), kind=kCustom, calls=%fused_computation.3.clone | custom fusion | bytes 540672 | tf_op jit(solution)/shard_map/jit(_take)/gather | solution.py:43
  118.3 4.9 %fusion.30 = (f32[4096]{0:T(1024)S(1)}, f32[16,4096]{0,1:T(8,128)}) fusion(f32[16,4096]{0,1:T(8,128)} %copy.23, f32[4096,16]{1,0:T(8,128)} %gather_fusion.3, pred[4096]{0:T(1024)(128)(4,1)S(1)} %compare_and_fusion, f32[16,4096]{0,1:T(8,128)S(1)} %get-tuple-element.107, f32[4096]{0:T(1024)S(1)} %add_multiply_fusion.3), kind=kLoop, calls=%fused_computation.60 | loop fusion | flops 454656 | bytes 1085440 | tf_op jit(solution)/shard_map/reduce_max | solution.py:13
  123.2 2.2 %copy.29 = f32[16,4096]{1,0:T(8,128)S(1)} copy(f32[16,4096]{0,1:T(8,128)} %get-tuple-element.105) | data formatting | bytes 524288 | tf_op jit(solution)/shard_map/while | solution.py:22
  125.4 4.1 %while.25 = (s32[]{:T(128)}, f32[4096]{0:T(1024)S(1)}, f32[4096]{0:T(1024)S(1)}, f32[16,4096]{1,0:T(8,128)S(1)}, s32[]{:T(128)}) while((s32[]{:T(128)}, f32[4096]{0:T(1024)S(1)}, f32[4096]{0:T(1024)S(1)}, f32[16,4096]{1,0:T(8,128)S(1)}, s32[]{:T(128)}) %tuple.57), condition=%wide.region_10.13_spmd, body=%wide.region_8.12_spmd.sunk | while | flops 229378 | bytes 499773 | solution.py:22
  129.5 25.5 %scatter_custom_fusion.2 = f32[1024,16]{1,0:T(8,128)S(1)} fusion(s32[4096]{0:T(1024)S(1)} %copy-done.4, f32[16,4096]{0,1:T(8,128)S(1)} %get-tuple-element.107, f32[]{:T(128)} %constant.48.clone.1, f32[]{:T(128)} %constant.10.clone.1, f32[4096]{0:T(1024)S(1)} %add_multiply_fusion.3, f32[16,4096]{0,1:T(8,128)} %get-tuple-element.105, ...), kind=kCustom, calls=%fused_computation.18 | custom fusion | flops 458752 | bytes 4294144 | tf_op jit(solution)/shard_map/scatter-add | solution.py:45
  155.3 5.8 %all_gather.7 = f32[4,8,2048]{2,1,0:T(8,128)S(1)} all-gather(f32[1,8,2048]{2,1,0:T(8,128)S(1)} %all_gather_reshape.7), channel_id=1, replica_groups=mesh['region'=8,'rep'=4] {'rep'}, dimensions={0}, use_global_device_ids=true | all-gather | bytes 327680 | tf_op jit(solution)/shard_map/all_gather | solution.py:49
  161.1 0.7 all_to_all.30
  161.7 3.3 %all-to-all-start.3 = ((f32[8,1,2048]{2,1,0:T(1,128)}), f32[8,1,2048]{2,1,0:T(1,128)S(1)}, u32[]{:S(2)}, u32[]{:S(2)}) async-start(f32[8,1,2048]{2,1,0:T(1,128)} %all_to_all.30), calls=%async_computation.3 | async-start | bytes 131072 | tf_op jit(solution)/shard_map/all_to_all | solution.py:50
  165.1 1.9 %subtract_maximum_fusion = f32[16,4096]{0,1:T(8,128)S(1)} fusion(f32[16,4096]{0,1:T(8,128)} %get-tuple-element.105, f32[4096]{0:T(1024)S(1)} %add_multiply_fusion.2), kind=kLoop, calls=%fused_computation.30 | loop fusion | flops 131072 | bytes 540672 | tf_op jit(solution)/shard_map/max | solution.py:24
  167.0 1.3 copy.30
  168.3 3.6 %all-to-all-done.3 = f32[8,1,2048]{2,1,0:T(1,128)S(1)} async-done(((f32[8,1,2048]{2,1,0:T(1,128)}), f32[8,1,2048]{2,1,0:T(1,128)S(1)}, u32[]{:S(2)}, u32[]{:S(2)}) %all-to-all-start.3) | async-done | bytes 65568 | tf_op jit(solution)/shard_map/all_to_all | solution.py:50
  172.3 6.2 %scatter_custom_fusion.3 = f32[512,16]{1,0:T(8,128)S(1)} fusion(s32[1024]{0:T(1024)} %bitcast.24, f32[1024,16]{1,0:T(8,128)S(1)} %reshape.126, f32[]{:T(128)} %constant.10.clone.1), kind=kCustom, calls=%fused_computation.44 | custom fusion | flops 16384 | bytes 33280 | tf_op jit(solution)/shard_map/scatter-add | solution.py:51
  178.6 0.6 add_maximum_fusion
  (336 shorter events, 8.2 us)
Async XLA Ops:
  2.9 11.2 %copy-start.4 = (s32[4096]{0:T(1024)S(1)}, s32[4096]{0:T(1024)}, u32[]{:S(2)}) copy-start(s32[4096]{0:T(1024)} %param.18) | copy-start | bytes 49156
  2.9 11.2 %copy-start = (f32[16,4096]{1,0:T(8,128)S(1)}, f32[16,4096]{1,0:T(8,128)}, u32[]{:S(2)}) copy-start(f32[16,4096]{1,0:T(8,128)} %param.14) | copy-start | bytes 786436
  5.7 10.4 %copy-start.1 = (f32[16,4096]{1,0:T(8,128)S(1)}, f32[16,4096]{1,0:T(8,128)}, u32[]{:S(2)}) copy-start(f32[16,4096]{1,0:T(8,128)} %param.15) | copy-start | bytes 786436
  6.8 14.2 %all-to-all-start = ((f32[8,1,2048]{2,1,0:T(1,128)}), f32[8,1,2048]{2,1,0:T(1,128)S(1)}, u32[]{:S(2)}, u32[]{:S(2)}) async-start(f32[8,1,2048]{2,1,0:T(1,128)} %all_to_all.32), calls=%async_computation | async-start | bytes 131072 | tf_op jit(solution)/shard_map/all_to_all | solution.py:41
  68.6 22.6 %copy-start.2 = (f32[8192]{0:T(1024)S(1)}, f32[8192]{0:T(1024)}, u32[]{:S(2)}) copy-start(f32[8192]{0:T(1024)} %param.16) | copy-start | bytes 98308
  68.6 22.6 %copy-start.3 = (f32[8192]{0:T(1024)S(1)}, f32[8192]{0:T(1024)}, u32[]{:S(2)}) copy-start(f32[8192]{0:T(1024)} %param.17) | copy-start | bytes 98308
  161.7 10.2 %all-to-all-start.3 = ((f32[8,1,2048]{2,1,0:T(1,128)}), f32[8,1,2048]{2,1,0:T(1,128)S(1)}, u32[]{:S(2)}, u32[]{:S(2)}) async-start(f32[8,1,2048]{2,1,0:T(1,128)} %all_to_all.30), calls=%async_computation.3 | async-start | bytes 131072 | tf_op jit(solution)/shard_map/all_to_all | solution.py:50
